TPU v7x, 128 devices: a whole 4x4x4 slice. The times are simulated.
128 devices in a mesh: dp: 16 (over x, z), pipe: 4 (over y_lo, core), tensor: 2 (over y_hi).
Axes of the slice: x: 4, y: 4 (y_hi: 2, y_lo: 2; y = y_hi * 2 + y_lo), z: 4, core: 2. Of those that a mesh axis runs over, the one named last changes fastest.
Arguments:
- stream: bfloat16 [4, 4096, 8192], P('pipe', 'dp', 'tensor'), as said below
- backup_stream: bfloat16 [4, 4096, 8192], P('pipe', 'dp', 'tensor'), as said below
- norm_gain: float32 [8192], P('tensor'), may hold values from 0.5 to 2
- w_key: bfloat16 [4, 8192, 1024], P('pipe', None, 'tensor'), may hold values from -0.0625 to 0.0625
- w_value: bfloat16 [4, 8192, 1024], P('pipe', None, 'tensor'), may hold values from -0.0625 to 0.0625
- key_cot: bfloat16 [4, 4096, 1024], P('pipe', 'dp', 'tensor'), as said below
- value_cot: bfloat16 [4, 4096, 1024], P('pipe', 'dp', 'tensor'), as said below
- backup_key_cot: bfloat16 [4, 4096, 1024], P('pipe', 'dp', 'tensor'), as said below
- backup_value_cot: bfloat16 [4, 4096, 1024], P('pipe', 'dp', 'tensor'), as said below
- positions: int32 [4, 4096], P('pipe'), may hold values from 0 to 4095, as said below
- failed: int32 [4], replicated, may hold values from 0 to 15, as said below
- reroute_plan: int32 [4, 32], replicated, may hold values from 0 to 15, as said below
Outputs:
- grad_key: float32 [4, 8192, 1024], P('pipe', 'dp', 'tensor')
- grad_value: float32 [4, 8192, 1024], P('pipe', 'dp', 'tensor')
- stream_grad: bfloat16 [4, 4096, 8192], P('pipe', 'dp', 'tensor')
- spill_grad: bfloat16 [4, 768, 8192], P('pipe', 'dp', 'tensor')
Inputs may be any that keep to these rules, and one draw needn't show every extreme that they name: failed[s] is the replica of section s that has failed; some section has lost replica 0 and some other section replica 16 - 1. reroute_plan[s, b] never equals failed[s]; every other replica takes at least one block of each section, none more than 6, and some replica takes exactly 6. positions count from 0 at each document start; documents of a section's rows start at least every 4096 rows, and in some section exactly every 4096 rows. In stream[j] the rows of replica failed[(j + 1) mod 4] are zero. In backup_stream[s] only the rows of replica (failed[s] + 1) mod 16 are nonzero. In key_cot[s] the rows of replica failed[s] are zero. In value_cot[s] the rows of replica failed[s] are zero. In backup_key_cot[s] only the rows of replica (failed[s] + 1) mod 16 are nonzero. In backup_value_cot[s] only the rows of replica (failed[s] + 1) mod 16 are nonzero.
All inputs are finite; a program needn't handle non-finite values.
Results may differ from a plain program's by a relative error of at most 0.015.
Values may be sent and summed in bfloat16 or wider, within the bound.
No kernel may reach another device: no remote copies, remote signals or barrier semaphores. Data moves between devices by JAX's collectives and lax.ppermute only.
A program may use at most 128 MiB of HBM per device.

v0:
```python
import math
import jax
import jax.numpy as jnp
from jax import lax
from jax.sharding import PartitionSpec as P

D = 8192
HEAD = 128
BLOCK = 8
EPSILON = 1e-05
ROPE_BASE = 500000.0


def passed_along(block, axis, distance):
    devices = range(lax.axis_size(axis))
    route = [((i - distance) % len(devices), i) for i in devices]
    return lax.ppermute(block, axis, route)


def broadcast(shard, axis, root):
    mine = lax.axis_index(axis) == root
    return lax.psum(jnp.where(mine, shard, jnp.zeros_like(shard)), axis)


def frequencies():
    index_half = jnp.arange(HEAD // 2, dtype=jnp.float32)
    return jnp.exp(-(2.0 * index_half / HEAD) * math.log(ROPE_BASE))


def derotate(cotangent, position):
    row_count = cotangent.shape[0]
    pieces = cotangent.astype(jnp.float32).reshape(row_count, -1, 2, HEAD // 2)
    angles = position.astype(jnp.float32)[:, None] * frequencies()[None, :]
    cosine = jnp.cos(angles)[:, None, :]
    sine_values = jnp.sin(angles)[:, None, :]
    lower_half = pieces[:, :, 0, :]
    upper_half = pieces[:, :, 1, :]
    new_lower = lower_half * cosine + upper_half * sine_values
    new_upper = upper_half * cosine - lower_half * sine_values
    return jnp.stack([new_lower, new_upper], axis=2).reshape(row_count, -1).astype(jnp.bfloat16)


def slot_rows(plan_row, owners, capacity_blocks, block_size):
    block_count = plan_row.shape[0]
    block_ids = jnp.arange(block_count, dtype=jnp.int32)
    same_owner = plan_row[:, None] == plan_row[None, :]
    earlier = block_ids[None, :] < block_ids[:, None]
    block_rank = jnp.sum(jnp.where(same_owner & earlier, 1, 0), axis=1).astype(jnp.int32)
    slot_ids = jnp.arange(capacity_blocks, dtype=jnp.int32)
    matches = (plan_row[None, None, :] == owners[:, None, None]) & (
        block_rank[None, None, :] == slot_ids[None, :, None]
    )
    chosen = jnp.sum(jnp.where(matches, block_ids[None, None, :], 0), axis=2)
    filled = jnp.any(matches, axis=2)
    offsets = jnp.arange(block_size, dtype=jnp.int32)
    indices = (chosen[:, :, None] * block_size + offsets[None, None, :]).reshape(
        owners.shape[0], -1
    )
    occupied = jnp.repeat(filled, block_size, axis=1)
    return (indices, occupied)


def on_device(
    stream,
    backup_stream,
    norm_gain,
    w_key,
    w_value,
    key_cot,
    value_cot,
    backup_key_cot,
    backup_value_cot,
    positions,
    failed,
    reroute_plan,
):
    section_idx = lax.axis_index("pipe")
    member = lax.axis_index("dp")
    replicas = lax.axis_size("dp")
    fallen = failed[section_idx]
    keeper = (fallen + 1) % replicas
    plan_row = reroute_plan[section_idx]
    blocks = plan_row.shape[0]
    own_rows = stream.shape[1]
    capacity_blocks = 2 * ((blocks + replicas - 2) // (replicas - 1))
    incoming = passed_along(stream[0], "pipe", 1)
    own_positions = lax.dynamic_slice_in_dim(positions[0], member * own_rows, own_rows, 0)
    dead_positions = lax.dynamic_slice_in_dim(positions[0], fallen * own_rows, own_rows, 0)
    cot_key = derotate(key_cot[0], own_positions)
    cot_both = jnp.concatenate([cot_key, value_cot[0]], axis=1)
    saved_key = derotate(backup_key_cot[0], dead_positions)
    saved_both = jnp.concatenate([saved_key, backup_value_cot[0]], axis=1)
    dead_rows, dead_cots = (
        broadcast(backup_stream[0], "dp", keeper),
        broadcast(saved_both, "dp", keeper),
    )
    indices, occupied = slot_rows(plan_row, jnp.reshape(member, (1,)), capacity_blocks, BLOCK)
    index_list = indices[0]
    keep_slot = occupied[0][:, None]
    survives = member != fallen

    def combine(mine, far_rows):
        picked = jnp.where(
            keep_slot, jnp.take(far_rows, index_list, axis=0), jnp.zeros((), far_rows.dtype)
        )
        kept = jnp.where(survives, mine, jnp.zeros((), mine.dtype))
        return jnp.concatenate([kept, picked], axis=0)

    inputs = combine(incoming, dead_rows)
    cots = combine(cot_both, dead_cots)
    key_width = w_key.shape[2]
    values = inputs.astype(jnp.float32)
    squares = lax.psum(jnp.sum(values * values, axis=1), "tensor")
    scales = lax.rsqrt(squares / D + EPSILON)
    normed = (values * scales[:, None] * norm_gain).astype(jnp.bfloat16)
    partial_sum = lax.dot_general(
        lax.all_gather(normed, "tensor", axis=1, tiled=True),
        cots,
        (((0,), (0,)), ((), ())),
        preferred_element_type=jnp.float32,
    )
    weight_sum = lax.psum_scatter(
        partial_sum.astype(jnp.bfloat16), "dp", scatter_dimension=0, tiled=True
    ).astype(jnp.float32)
    contract = (((1,), (1,)), ((), ()))
    feature = lax.dot_general(
        cots[:, :key_width], w_key[0], contract, preferred_element_type=jnp.float32
    )
    feature = feature + lax.dot_general(
        cots[:, key_width:], w_value[0], contract, preferred_element_type=jnp.float32
    )
    feature_part = lax.psum_scatter(
        feature.astype(jnp.bfloat16), "tensor", scatter_dimension=1, tiled=True
    ).astype(jnp.float32)
    scaled = norm_gain * feature_part
    input_grad = (scales[:, None] * scaled).astype(jnp.bfloat16)
    returned = passed_along(input_grad, "pipe", -1)
    own_count = returned.shape[0] - index_list.shape[0]
    return (
        weight_sum[:, :key_width][None],
        weight_sum[:, key_width:][None],
        returned[:own_count][None],
        returned[own_count:][None],
    )


def solution(mesh):
    return jax.shard_map(
        on_device,
        mesh=mesh,
        in_specs=(
            P("pipe", "dp", "tensor"),
            P("pipe", "dp", "tensor"),
            P("tensor"),
            P("pipe", None, "tensor"),
            P("pipe", None, "tensor"),
            P("pipe", "dp", "tensor"),
            P("pipe", "dp", "tensor"),
            P("pipe", "dp", "tensor"),
            P("pipe", "dp", "tensor"),
            P("pipe", None),
            P(),
            P(),
        ),
        out_specs=(
            P("pipe", "dp", "tensor"),
            P("pipe", "dp", "tensor"),
            P("pipe", "dp", "tensor"),
            P("pipe", "dp", "tensor"),
        ),
        check_vma=False,
    )
```

profile of v0, /device:TPU:1, one launch (start us, length us, event | category | flops | bytes accessed | tf_op | source)
XLA Modules:
  0.0 429.3 jit_solution(5361297684138172872)
XLA Ops:
  7.2 1.4 dynamic_slice.12
  10.0 1.1 copy.21
  11.1 1.1 copy.23
  12.2 0.7 dynamic-slice_convert_fusion.1
  12.9 0.5 multiply_cosine_fusion.1
  13.5 0.1 add_convert_fusion
  13.7 0.1 copy.24
  13.8 1.5 select_bitcast_fusion
  15.3 1.9 maximum_select_fusion.1
  17.9 0.7 broadcast_compare_fusion
  18.6 0.2 select_reduce_fusion
  18.7 0.2 select_reduce_fusion.1
  19.0 0.1 add.107
  19.0 0.1 add.116
  19.1 0.1 add.108
  19.2 0.2 fusion.13
  19.4 0.1 broadcast_in_dim.115
  19.5 0.1 broadcast_in_dim.116
  19.6 0.1 add.118
  19.7 0.1 add.110
  19.8 0.1 copy.22
  20.0 0.1 maximum_select_fusion
  20.1 93.1 %all-reduce.3.cloned.1.call-done = (bf16[256,4096]{1,0:T(8,128)(2,1)}, bf16[256,1024]{1,0:T(8,128)(2,1)}) async-done(((bf16[256,4096]{1,0:T(8,128)(2,1)}, bf16[256,1024]{1,0:T(8,128)(2,1)}), (bf16[256,4096]{1,0:T(8,128)(2,1)}, bf16[256,1024]{1,0:T(8,128)(2,1)})) %all-reduce.3.cloned.1.call-update) | async-done | bytes 2621456 | tf_op jit(solution)/shard_map/psum | solution.py:22
  113.2 1.8 gather_fusion.1
  115.0 0.1 select_select_fusion.1
  115.1 11.4 %fusion.2 = f32[304,8192]{1,0:T(8,128)} fusion(bf16[1,8192,512]{2,1,0:T(8,128)(2,1)} %param.15, bf16[256,1024]{1,0:T(8,128)(2,1)S(1)} %maximum_select_fusion, bf16[48,1024]{1,0:T(8,128)(2,1)S(1)} %select_select_fusion.1), kind=kOutput, calls=%fused_computation.6 | convolution fusion | flops 2550759424 | bytes 18972672 | tf_op jit(solution)/shard_map/dot_general | solution.py:126
  126.5 12.1 %fusion = bf16[304,8192]{1,0:T(8,128)(2,1)} fusion(f32[304,8192]{1,0:T(8,128)} %fusion.2, bf16[1,8192,512]{2,1,0:T(8,128)(2,1)} %param.16, bf16[256,1024]{1,0:T(8,128)(2,1)S(1)} %maximum_select_fusion, bf16[48,1024]{1,0:T(8,128)(2,1)S(1)} %select_select_fusion.1), kind=kOutput, calls=%fused_computation.4 | convolution fusion | flops 2555740160 | bytes 23953408 | tf_op jit(solution)/shard_map/dot_general | solution.py:129
  138.7 1.5 copy-done.4
  140.2 2.1 collective-permute-start
  142.4 59.5 %collective-permute-done = bf16[256,4096]{1,0:T(8,128)(2,1)S(1)} collective-permute-done((bf16[256,4096]{1,0:T(8,128)(2,1)S(1)}, bf16[256,4096]{1,0:T(8,128)(2,1)S(1)}, u32[]{:S(2)}, u32[]{:S(2)}) %collective-permute-start) | collective-permute-done | bytes 2097184 | tf_op jit(solution)/shard_map/ppermute | solution.py:17
  201.8 0.1 broadcast_select_fusion
  201.9 3.0 gather_fusion
  205.0 0.1 select_select_fusion
  205.1 0.6 fusion.4
  205.7 5.7 %psum.22 = f32[304]{0:T(512)S(1)} all-reduce(f32[304]{0:T(512)S(1)} %fusion.4), channel_id=1, replica_groups=mesh['dp'=16,'pipe'=4,'tensor'=2] {'tensor'}, use_global_device_ids=true, to_apply=%region_5.6 | all-reduce | flops 304 | bytes 2432 | tf_op jit(solution)/shard_map/psum | solution.py:113
  211.5 12.0 %reduce-scatter.5.cloned.1.call-done = bf16[304,4096]{1,0:T(8,128)(2,1)} async-done(((bf16[304,8192]{1,0:T(8,128)(2,1)}), bf16[304,4096]{1,0:T(8,128)(2,1)}) %reduce-scatter.5.cloned.1.call-update) | async-done | bytes 2490384 | tf_op jit(solution)/shard_map/reduce_scatter | solution.py:132
  223.4 4.9 %multiply_convert_fusion = (bf16[304,4096]{1,0:T(8,128)(2,1)}, bf16[304,4096]{1,0:T(8,128)(2,1)}) fusion(bf16[304,4096]{1,0:T(8,128)(2,1)} %reduce-scatter.5.cloned.1.call-done, f32[4096]{0:T(1024)S(1)} %copy-done.3, f32[304]{0:T(512)S(1)} %add_rsqrt_fusion, bf16[48,4096]{1,0:T(8,128)(2,1)S(1)} %select_select_fusion, ...), kind=kLoop, calls=%fused_computation.13 | loop fusion | flops 13697024 | bytes 9979072 | tf_op jit(solution)/shard_map/convert_element_type | solution.py:136
  228.3 0.2 reduce-scatter.3.cloned.1.call-start
  228.5 66.4 %all-gather.2.cloned.1.call-done = bf16[304,8192]{1,0:T(8,128)(2,1)} async-done(((bf16[304,4096]{1,0:T(8,128)(2,1)}), bf16[304,8192]{1,0:T(8,128)(2,1)}) %all-gather.2.cloned.1.call-update) | async-done | bytes 4980752 | tf_op jit(solution)/shard_map/all_gather | solution.py:117
  294.9 14.9 %convolution_convert_fusion = bf16[8192,1024]{1,0:T(8,128)(2,1)} fusion(bf16[304,8192]{1,0:T(8,128)(2,1)} %all-gather.2.cloned.1.call-done, bf16[48,1024]{1,0:T(8,128)(2,1)S(1)} %select_select_fusion.1, bf16[256,1024]{1,0:T(8,128)(2,1)S(1)} %maximum_select_fusion), kind=kOutput, calls=%fused_computation.2 | convolution fusion | flops 5109907456 | bytes 22380544 | tf_op jit(solution)/shard_map/dot_general | solution.py:116
  309.9 1.7 copy-done
  311.6 0.7 collective-permute-start.1
  312.2 29.4 %collective-permute-done.1 = bf16[304,4096]{1,0:T(8,128)(2,1)S(1)} collective-permute-done((bf16[304,4096]{1,0:T(8,128)(2,1)S(1)}, bf16[304,4096]{1,0:T(8,128)(2,1)S(1)}, u32[]{:S(2)}, u32[]{:S(2)}) %collective-permute-start.1) | collective-permute-done | bytes 2490400 | tf_op jit(solution)/shard_map/ppermute | solution.py:17
  341.6 0.8 slice_bitcast_fusion.3
  342.4 1.5 slice_bitcast_fusion
  343.8 76.0 %reduce-scatter.3.cloned.1.call-done = bf16[512,1024]{1,0:T(8,128)(2,1)} async-done(((bf16[8192,1024]{1,0:T(8,128)(2,1)}), bf16[512,1024]{1,0:T(8,128)(2,1)}) %reduce-scatter.3.cloned.1.call-update) | async-done | bytes 1048592 | tf_op jit(solution)/shard_map/reduce_scatter | solution.py:122
  419.8 1.5 convert_element_type.76
  421.3 1.5 slice_bitcast_fusion.1
  (27 shorter events, 0.4 us)
Async XLA Ops:
  7.2 6.7 %copy-start.1 = (bf16[1,256,4096]{2,1,0:T(8,128)(2,1)S(1)}, bf16[1,256,4096]{2,1,0:T(8,128)(2,1)}, u32[]{:S(2)}) copy-start(bf16[1,256,4096]{2,1,0:T(8,128)(2,1)} %param.13) | copy-start | bytes 6291460
  7.2 106.0 %all-reduce.3.cloned.1.call-start = ((), (), s32[]{:S(2)}) async-start(), calls=%async_computation.5 | async-start | bytes 5242880 | tf_op jit(solution)/shard_map/psum | solution.py:22
  13.6 6.3 %copy-start.2 = (bf16[1,256,512]{2,1,0:T(8,128)(2,1)S(1)}, bf16[1,256,512]{2,1,0:T(8,128)(2,1)}, u32[]{:S(2)}) copy-start(bf16[1,256,512]{2,1,0:T(8,128)(2,1)} %param.18) | copy-start | bytes 786436
  17.2 206.2 %reduce-scatter.5.cloned.1.call-start = ((), (), s32[]{:S(2)}) async-start(), calls=%async_computation.4 | async-start | bytes 7471104 | tf_op jit(solution)/shard_map/reduce_scatter | solution.py:132
  138.6 1.6 copy-start.4
  138.6 156.3 %all-gather.2.cloned.1.call-start = ((), (), s32[]{:S(2)}) async-start(), calls=%async_computation.2 | async-start | bytes 7471104 | tf_op jit(solution)/shard_map/all_gather | solution.py:117
  140.2 83.2 %copy-start.3 = (f32[4096]{0:T(1024)S(1)}, f32[4096]{0:T(1024)}, u32[]{:S(2)}) copy-start(f32[4096]{0:T(1024)} %param.14) | copy-start | bytes 49156
  140.2 61.6 %collective-permute-start = (bf16[256,4096]{1,0:T(8,128)(2,1)S(1)}, bf16[256,4096]{1,0:T(8,128)(2,1)S(1)}, u32[]{:S(2)}, u32[]{:S(2)}) collective-permute-start(bf16[256,4096]{1,0:T(8,128)(2,1)S(1)} %bitcast.46), channel_id=1, source_target_pairs={{6,0},{0,2},{2,4},{4,6},{7,1},{1,3},{3,5},{5,7},{14,8},{8,10},{10,... | collective-permute-start | bytes 6291464 | tf_op jit(solution)/shard_map/ppermute | solution.py:17
  228.3 191.5 %reduce-scatter.3.cloned.1.call-start = ((), (), s32[]{:S(2)}) async-start(), calls=%async_computation.3 | async-start | bytes 17825792 | tf_op jit(solution)/shard_map/reduce_scatter | solution.py:122
  309.8 1.7 copy-start
  311.6 30.1 %collective-permute-start.1 = (bf16[304,4096]{1,0:T(8,128)(2,1)S(1)}, bf16[304,4096]{1,0:T(8,128)(2,1)S(1)}, u32[]{:S(2)}, u32[]{:S(2)}) collective-permute-start(bf16[304,4096]{1,0:T(8,128)(2,1)S(1)} %copy-done), channel_id=1, source_target_pairs={{2,0},{4,2},{6,4},{0,6},{3,1},{5,3},{7,5},{1,7},{10,8},{12,10},{14... | collective-permute-start | bytes 7471112 | tf_op jit(solution)/shard_map/ppermute | solution.py:17
Sparse Core Ops, SparseCore 0:
  17.3 95.8 all-reduce.2
  138.8 84.5 reduce-scatter.4
  228.4 66.4 all-gather.1
  310.0 109.7 reduce-scatter.2
where the time goes:
time: 430 us; the launch traced here: 429 us
  waiting for transfers between devices  336 us (78%)
  matrix products  38.4 us (9%)
  local copies, waits for them, and re-layouts  16.2 us (4%)
  between operations  16 us (4%)
  other arithmetic  13.5 us (3%)
  blocking collectives  5.75 us (1%)
    psum x1, waiting for transfers between devices, broadcast(): return lax.psum(jnp.where(mine, shard, jnp.zeros_like(shard)), axis)  93.1 us
    ppermute x2, waiting for transfers between devices, passed_along(): return lax.ppermute(block, axis, route)  88.9 us
    reduce_scatter x1, waiting for transfers between devices, on_device(): lax.psum_scatter(partial_sum.astype(jnp.bfloat16), 'dp', scatter_dimensio...  76 us
    all_gather x1, waiting for transfers between devices, on_device(): lax.all_gather(normed, 'tensor', axis=1, tiled=True)  66.4 us
    dot_general x1, matrix products, on_device(): lax.dot_general(lax.all_gather(normed, 'tensor', axis=1, tiled=True), cot...  14.9 us
    dot_general x1, matrix products, on_device(): lax.dot_general(cots[:, key_width:], w_value[0], contract, preferred_elem...  12.1 us
    reduce_scatter x1, waiting for transfers between devices, on_device(): lax.psum_scatter(feature.astype(jnp.bfloat16), 'tensor', scatter_dimensio...  12 us
    dot_general x1, matrix products, on_device(): lax.dot_general(cots[:, :key_width], w_key[0], contract, preferred_elemen...  11.4 us
  transfers between devices with their start and end apart: 6, of which 6 were waited for; matrix products, arithmetic and copies ran while one was open for 2% of the time, Pallas kernels for 0%

commit v1 on v0

--- a/solution.py
+++ b/solution.py
@@ -19,7 +19,7 @@
 
 def broadcast(shard, axis, root):
     mine = lax.axis_index(axis) == root
-    return lax.psum(jnp.where(mine, shard, jnp.zeros_like(shard)), axis)
+    return jnp.sum(lax.all_gather(jnp.where(mine, shard, jnp.zeros_like(shard)), axis), axis=0)
 
 
 def frequencies():

time: 430 us -> 569 us (1.32)
  waiting for transfers between devices: 336 us -> 454 us
  other arithmetic: 13.5 us -> 31.9 us
    all_gather x0 -> x2, waiting for transfers between devices: none -> 212 us  [broadcast(): lax.all_gather(jnp.where(mine, shard, jnp.zeros_like(shard)), axis)]
    psum x1 -> x0, waiting for transfers between devices: 93.1 us -> none  [broadcast(): return lax.psum(jnp.where(mine, shard, jnp.zeros_like(shard)), axis)]
    ppermute x2, waiting for transfers between devices: 88.9 us -> 52.4 us  [passed_along(): return lax.ppermute(block, axis, route)]
    reduce_scatter x1, waiting for transfers between devices: 12 us -> 44.8 us  [on_device(): lax.psum_scatter(feature.astype(jnp.bfloat16), 'tensor', scatter_dimensio...]
    reduce_sum x0 -> x2, other arithmetic: none -> 18.4 us  [broadcast(): jnp.sum(lax.all_gather(jnp.where(mine, shard, jnp.zeros_like(shard)), axi...]
  transfers between devices with their start and end apart: 6 -> 7, of which waited for: 6 -> 7; matrix products, arithmetic and copies ran while one was open for 2% -> 10% of each run, Pallas kernels for 0% -> 0%
where the time goes in v1:
time: 569 us; the launch traced here: 568 us
  waiting for transfers between devices  454 us (80%)
  matrix products  38.8 us (7%)
  other arithmetic  31.9 us (6%)
  local copies, waits for them, and re-layouts  18.9 us (3%)
  between operations  16 us (3%)
  blocking collectives  5.75 us (1%)
    all_gather x2, waiting for transfers between devices, broadcast(): lax.all_gather(jnp.where(mine, shard, jnp.zeros_like(shard)), axis)  212 us
    reduce_scatter x1, waiting for transfers between devices, on_device(): lax.psum_scatter(partial_sum.astype(jnp.bfloat16), 'dp', scatter_dimensio...  75.9 us
    all_gather x1, waiting for transfers between devices, on_device(): lax.all_gather(normed, 'tensor', axis=1, tiled=True)  69.2 us
    ppermute x2, waiting for transfers between devices, passed_along(): return lax.ppermute(block, axis, route)  52.4 us
    reduce_scatter x1, waiting for transfers between devices, on_device(): lax.psum_scatter(feature.astype(jnp.bfloat16), 'tensor', scatter_dimensio...  44.8 us
    reduce_sum x2, other arithmetic, broadcast(): jnp.sum(lax.all_gather(jnp.where(mine, shard, jnp.zeros_like(shard)), axi...  18.4 us
    dot_general x1, matrix products, on_device(): lax.dot_general(lax.all_gather(normed, 'tensor', axis=1, tiled=True), cot...  15 us
    dot_general x1, matrix products, on_device(): lax.dot_general(cots[:, key_width:], w_value[0], contract, preferred_elem...  12.4 us
  transfers between devices with their start and end apart: 7, of which 7 were waited for; matrix products, arithmetic and copies ran while one was open for 10% of the time, Pallas kernels for 0%

profile of v1, /device:TPU:1, one launch (start us, length us, event | category | flops | bytes accessed | tf_op | source)
XLA Modules:
  0.0 567.9 jit_solution(16384293832523765125)
XLA Ops:
  7.2 1.4 dynamic_slice.12
  10.0 1.1 copy.30
  11.1 1.1 copy.32
  12.2 1.1 copy.33
  13.3 0.7 dynamic-slice_convert_fusion.1
  14.0 0.5 multiply_cosine_fusion.1
  14.6 0.8 add_convert_fusion
  15.4 0.1 maximum_select_fusion.1
  15.5 1.0 copy.34
  16.6 1.5 broadcast_select_fusion
  18.8 0.7 broadcast_compare_fusion
  19.5 0.2 select_reduce_fusion
  19.6 0.2 select_reduce_fusion.1
  19.9 0.1 add.112
  20.1 0.2 fusion.12
  20.4 0.1 broadcast_in_dim.118
  20.6 0.1 add.106
  20.6 1.1 copy.31
  21.8 0.1 maximum_select_fusion
  21.9 68.8 %all-gather.8.cloned.1.call-done = bf16[16,256,1024]{2,1,0:T(8,128)(2,1)} async-done(((bf16[1,256,1024]{2,1,0:T(8,128)(2,1)}), bf16[16,256,1024]{2,1,0:T(8,128)(2,1)}) %all-gather.8.cloned.1.call-update) | async-done | bytes 8388624 | tf_op jit(solution)/shard_map/all_gather | solution.py:22
  90.8 5.4 reduce_sum.55
  96.2 0.7 gather_fusion.1
  96.9 0.1 select_select_fusion.1
  97.0 0.2 copy.37
  97.1 11.4 %fusion.2 = f32[304,8192]{1,0:T(8,128)} fusion(bf16[1,8192,512]{2,1,0:T(8,128)(2,1)} %param.15, bf16[256,1024]{0,1:T(8,128)(2,1)S(1)} %maximum_select_fusion, bf16[48,1024]{0,1:T(8,128)(2,1)S(1)} %copy.37), kind=kOutput, calls=%fused_computation.6 | convolution fusion | flops 2550759424 | bytes 18972672 | tf_op jit(solution)/shard_map/dot_general | solution.py:126
  108.6 12.4 %fusion = bf16[304,8192]{1,0:T(8,128)(2,1)} fusion(f32[304,8192]{1,0:T(8,128)} %fusion.2, bf16[1,8192,512]{2,1,0:T(8,128)(2,1)} %param.16, bf16[256,1024]{0,1:T(8,128)(2,1)S(1)} %maximum_select_fusion, bf16[48,1024]{0,1:T(8,128)(2,1)S(1)} %copy.37), kind=kOutput, calls=%fused_computation.4 | convolution fusion | flops 2555740160 | bytes 23953408 | tf_op jit(solution)/shard_map/dot_general | solution.py:129
  121.0 1.6 copy-done.4
  122.6 1.7 collective-permute-start
  124.3 23.0 %collective-permute-done = bf16[256,4096]{1,0:T(8,128)(2,1)S(1)} collective-permute-done((bf16[256,4096]{1,0:T(8,128)(2,1)S(1)}, bf16[256,4096]{1,0:T(8,128)(2,1)S(1)}, u32[]{:S(2)}, u32[]{:S(2)}) %collective-permute-start) | collective-permute-done | bytes 2097184 | tf_op jit(solution)/shard_map/ppermute | solution.py:17
  147.3 0.1 broadcast_select_fusion.1
  147.5 142.8 %all-gather.4.cloned.1.call-done = bf16[16,256,4096]{2,1,0:T(8,128)(2,1)} async-done(((bf16[1,256,4096]{2,1,0:T(8,128)(2,1)}), bf16[16,256,4096]{2,1,0:T(8,128)(2,1)}) %all-gather.4.cloned.1.call-update) | async-done | bytes 33554448 | tf_op jit(solution)/shard_map/all_gather | solution.py:22
  290.3 13.0 %reduce_sum.53 = bf16[256,4096]{1,0:T(8,128)(2,1)} reduce(bf16[16,256,4096]{2,1,0:T(8,128)(2,1)} %all-gather.4.cloned.1.call-done, bf16[]{:T(256)} %constant.70.clone.1), dimensions={0}, to_apply=%region_3.4 | reduce | flops 15728640 | bytes 35651584 | tf_op jit(solution)/shard_map/reduce_sum | solution.py:22
  303.3 3.8 gather_fusion
  307.0 1.1 select_select_fusion
  308.2 0.6 fusion.4
  308.7 5.7 %psum.7 = f32[304]{0:T(512)S(1)} all-reduce(f32[304]{0:T(512)S(1)} %fusion.4), channel_id=1, replica_groups=mesh['dp'=16,'pipe'=4,'tensor'=2] {'tensor'}, use_global_device_ids=true, to_apply=%region_5.6 | all-reduce | flops 304 | bytes 2432 | tf_op jit(solution)/shard_map/psum | solution.py:113
  314.5 44.8 %reduce-scatter.5.cloned.1.call-done = bf16[304,4096]{1,0:T(8,128)(2,1)} async-done(((bf16[304,8192]{1,0:T(8,128)(2,1)}), bf16[304,4096]{1,0:T(8,128)(2,1)}) %reduce-scatter.5.cloned.1.call-update) | async-done | bytes 2490384 | tf_op jit(solution)/shard_map/reduce_scatter | solution.py:132
  359.3 4.9 multiply_convert_fusion
  364.3 69.2 %all-gather.6.cloned.1.call-done = bf16[304,8192]{1,0:T(8,128)(2,1)} async-done(((bf16[304,4096]{1,0:T(8,128)(2,1)}), bf16[304,8192]{1,0:T(8,128)(2,1)}) %all-gather.6.cloned.1.call-update) | async-done | bytes 4980752 | tf_op jit(solution)/shard_map/all_gather | solution.py:117
  433.5 15.0 %convolution_convert_fusion = bf16[8192,1024]{1,0:T(8,128)(2,1)} fusion(bf16[304,8192]{1,0:T(8,128)(2,1)} %all-gather.6.cloned.1.call-done, bf16[48,1024]{0,1:T(8,128)(2,1)S(1)} %copy.37, bf16[256,1024]{0,1:T(8,128)(2,1)S(1)} %maximum_select_fusion), kind=kOutput, calls=%fused_computation.2 | convolution fusion | flops 5109907456 | bytes 22380544 | tf_op jit(solution)/shard_map/dot_general | solution.py:116
  448.5 1.7 copy-done
  450.2 0.7 collective-permute-start.1
  450.8 29.4 %collective-permute-done.1 = bf16[304,4096]{1,0:T(8,128)(2,1)S(1)} collective-permute-done((bf16[304,4096]{1,0:T(8,128)(2,1)S(1)}, bf16[304,4096]{1,0:T(8,128)(2,1)S(1)}, u32[]{:S(2)}, u32[]{:S(2)}) %collective-permute-start.1) | collective-permute-done | bytes 2490400 | tf_op jit(solution)/shard_map/ppermute | solution.py:17
  480.2 0.8 slice_bitcast_fusion.3
  481.0 1.5 slice_bitcast_fusion
  482.5 75.9 %reduce-scatter.3.cloned.1.call-done = bf16[512,1024]{1,0:T(8,128)(2,1)} async-done(((bf16[8192,1024]{1,0:T(8,128)(2,1)}), bf16[512,1024]{1,0:T(8,128)(2,1)}) %reduce-scatter.3.cloned.1.call-update) | async-done | bytes 1048592 | tf_op jit(solution)/shard_map/reduce_scatter | solution.py:122
  558.4 1.5 convert_element_type.83
  559.8 1.5 slice_bitcast_fusion.1
  (34 shorter events, 0.8 us)
Async XLA Ops:
  7.2 9.4 %copy-start.1 = (bf16[1,256,4096]{2,1,0:T(8,128)(2,1)S(1)}, bf16[1,256,4096]{2,1,0:T(8,128)(2,1)}, u32[]{:S(2)}) copy-start(bf16[1,256,4096]{2,1,0:T(8,128)(2,1)} %param.13) | copy-start | bytes 6291460
  7.2 83.6 %all-gather.8.cloned.1.call-start = ((), (), s32[]{:S(2)}) async-start(), calls=%async_computation.4 | async-start | bytes 8912896 | tf_op jit(solution)/shard_map/all_gather | solution.py:22
  15.4 6.4 %copy-start.2 = (bf16[256,4,1,64]{0,3,2,1:T(8,128)(2,1)S(1)}, bf16[256,4,1,64]{0,3,2,1:T(8,128)(2,1)}, u32[]{:S(2)}) copy-start(bf16[256,4,1,64]{0,3,2,1:T(8,128)(2,1)} %get-tuple-element.23) | copy-start | bytes 393220
  16.5 273.8 %all-gather.4.cloned.1.call-start = ((), (), s32[]{:S(2)}) async-start(), calls=%async_computation.2 | async-start | bytes 35651584 | tf_op jit(solution)/shard_map/all_gather | solution.py:22
  18.1 341.2 %reduce-scatter.5.cloned.1.call-start = ((), (), s32[]{:S(2)}) async-start(), calls=%async_computation.6 | async-start | bytes 7471104 | tf_op jit(solution)/shard_map/reduce_scatter | solution.py:132
  121.0 1.7 copy-start.4
  121.0 312.5 %all-gather.6.cloned.1.call-start = ((), (), s32[]{:S(2)}) async-start(), calls=%async_computation.3 | async-start | bytes 7471104 | tf_op jit(solution)/shard_map/all_gather | solution.py:117
  122.6 24.7 %collective-permute-start = (bf16[256,4096]{1,0:T(8,128)(2,1)S(1)}, bf16[256,4096]{1,0:T(8,128)(2,1)S(1)}, u32[]{:S(2)}, u32[]{:S(2)}) collective-permute-start(bf16[256,4096]{1,0:T(8,128)(2,1)S(1)} %bitcast.42), channel_id=1, source_target_pairs={{6,0},{0,2},{2,4},{4,6},{7,1},{1,3},{3,5},{5,7},{14,8},{8,10},{10,... | collective-permute-start | bytes 6291464 | tf_op jit(solution)/shard_map/ppermute | solution.py:17
  303.3 56.1 %copy-start.3 = (f32[4096]{0:T(1024)S(1)}, f32[4096]{0:T(1024)}, u32[]{:S(2)}) copy-start(f32[4096]{0:T(1024)} %param.14) | copy-start | bytes 49156
  364.3 194.1 %reduce-scatter.3.cloned.1.call-start = ((), (), s32[]{:S(2)}) async-start(), calls=%async_computation.5 | async-start | bytes 17825792 | tf_op jit(solution)/shard_map/reduce_scatter | solution.py:122
  448.5 1.7 copy-start
  450.2 30.1 %collective-permute-start.1 = (bf16[304,4096]{1,0:T(8,128)(2,1)S(1)}, bf16[304,4096]{1,0:T(8,128)(2,1)S(1)}, u32[]{:S(2)}, u32[]{:S(2)}) collective-permute-start(bf16[304,4096]{1,0:T(8,128)(2,1)S(1)} %copy-done), channel_id=1, source_target_pairs={{2,0},{4,2},{6,4},{0,6},{3,1},{5,3},{7,5},{1,7},{10,8},{12,10},{14... | collective-permute-start | bytes 7471112 | tf_op jit(solution)/shard_map/ppermute | solution.py:17
Sparse Core Ops, SparseCore 0:
  16.7 74.0 all-gather.7
  93.5 196.7 all-gather.3
  292.7 66.5 reduce-scatter.4
  364.4 69.0 all-gather.5
  448.6 109.7 reduce-scatter.2
